TPU v7x, 128 devices: a whole 4x4x4 slice. The times are simulated.
128 devices in a mesh: src: 8 (over z_lo, y), tgt: 16 (over x, z_hi, core).
Axes of the slice: x: 4, y: 4, z: 4 (z_hi: 2, z_lo: 2; z = z_hi * 2 + z_lo), core: 2. Of those that a mesh axis runs over, the one named last changes fastest.
Arguments:
- source_values: float32 [16, 1048576], P(None, ('src', 'tgt')), may hold values from -6 to 6
- source_phase: float32 [1048576], P(('src', 'tgt')), may hold values from -3.140625 to 3.140625
- leaf_interp: bfloat16 [64, 64], replicated, may hold values from -0.75 to 0.75
- level_interp: bfloat16 [13, 2, 64, 64], replicated, may hold values from -0.5 to 0.5
- level_phase: float32 [13, 3, 16384, 64], P(None, None, ('src', 'tgt')), may hold values from -3.140625 to 3.140625
- middle_interp: bfloat16 [64, 64], replicated, may hold values from -0.75 to 0.75
- middle_phase: float32 [2, 16384, 64], P(None, ('src', 'tgt')), may hold values from -3.140625 to 3.140625
- final_phase: float32 [16384, 64], P(('src', 'tgt')), may hold values from -3.140625 to 3.140625
- final_interp: bfloat16 [64, 64], replicated, may hold values from -0.75 to 0.75
- target_phase: float32 [1048576], P(('src', 'tgt')), may hold values from -3.140625 to 3.140625
Outputs:
- target_values: float32 [2, 16, 1048576], P(None, None, ('src', 'tgt'))
All inputs are finite; a program needn't handle non-finite values.
Results may differ from a plain program's by a relative error of at most 0.024.
Values may be sent and summed in bfloat16 or wider, within the bound.
No kernel may reach another device: no remote copies, remote signals or barrier semaphores. Data moves between devices by JAX's collectives and lax.ppermute only.
A program may use at most 64 MiB of HBM per device.

v0:
```python
import functools

import functools

import jax
import jax.numpy as jnp
from jax import lax
from jax.experimental import pallas as pl
from jax.experimental.pallas import tpu as pltpu
from jax.sharding import PartitionSpec as P

F32 = jnp.float32
BF16 = jnp.bfloat16
PAIRS = 16
E_PARTS = ((0, 1),)
D_PARTS = ((0, 1),)
SIN_FIT = (3.14159258, -5.16770688, 2.55003138, -0.59804517, 0.07722012)
COS_FIT = (0.99999995, -4.93479286, 4.05841191, -1.33188014, 0.21969675)


def cos_sin(theta):
    turns = theta * F32(0.15915494309189535)
    turns = turns - jnp.round(turns)
    square = turns * turns
    sin_half = F32(SIN_FIT[4])
    cos_half = F32(COS_FIT[4])
    for k in (3, 2, 1, 0):
        sin_half = sin_half * square + F32(SIN_FIT[k])
        cos_half = cos_half * square + F32(COS_FIT[k])
    sin_half = sin_half * turns
    twice = sin_half + sin_half
    return 1.0 - twice * sin_half, twice * cos_half


def iota(shape, axis):
    return lax.broadcasted_iota(jnp.int32, shape, axis)


def xor_partner(values, stride, axis):
    size = values.shape[axis]
    bit = (iota(values.shape, axis) & stride) != 0
    return jnp.where(
        bit, pltpu.roll(values, stride, axis), pltpu.roll(values, size - stride, axis)
    )


def dot_last(left, right):
    return lax.dot_general(left, right, (((1,), (1,)), ((), ())), preferred_element_type=F32)


def permutation(size, row_of):
    rows = iota((size, size), 0)
    columns = iota((size, size), 1)
    return jnp.where(columns == row_of(rows), 1.0, 0.0).astype(BF16)


def lower(shape):
    return iota(shape, 1) < 64


def halves(matrix):
    matrix = matrix.astype(F32)
    doubled = jnp.concatenate([matrix, matrix], 1)
    zeros = jnp.zeros_like(doubled)
    low = lower(doubled.shape)
    return (
        jnp.where(low, doubled, zeros).astype(BF16),
        jnp.where(low, zeros, doubled).astype(BF16),
        zeros.astype(BF16),
    )


def put_weights(weights, matrices):
    for n, matrix in enumerate(matrices):
        low, high, _ = halves(matrix)
        weights[128 * n : 128 * n + 64, :] = low
        weights[128 * n + 64 : 128 * n + 128, :] = high


def put_trig(theta, table):
    low = lower(theta.shape)
    for at, value in zip((0, 128), cos_sin(theta)):
        turned = pltpu.roll(value, 64, 1)
        table[:, at : at + 128] = jnp.where(low, value, turned)
        table[:, at + 256 : at + 384] = jnp.where(low, turned, value)


def put_single_trig(theta, table):
    cosine, sine = cos_sin(theta)
    table[:, 0:128] = cosine
    table[:, 128:256] = sine


def turn(table, row, at, tile):
    real, imag = tile
    cosine = table[row : row + 1, at : at + 128]
    sine = table[row : row + 1, at + 128 : at + 256]
    turned = jnp.concatenate([real * cosine - imag * sine, real * sine + imag * cosine], 0)
    return turned.astype(BF16)


def split(tile):
    tile = tile.astype(F32)
    return tile[0:8], tile[8:16]


def level(pairs, load, row_of, table, weights, left, store):
    for step in range(0, len(pairs), PAIRS):
        rows = left.at[(step // PAIRS) % 2]
        chunk = pairs[step : step + PAIRS]
        slots = []
        for pair in chunk:
            tiles = [split(load(slot)) for slot in pair]
            for slot, own, other in zip(pair, tiles, tiles[::-1]):
                span = slice(16 * len(slots), 16 * len(slots) + 16)
                rows[span, 0:128] = turn(table, row_of(slot), 0, own)
                rows[span, 128:256] = turn(table, row_of(slot), 256, other)
                slots.append(slot)
        size = 16 * len(slots)
        product = jnp.dot(rows[:size, :], weights[...], preferred_element_type=F32).astype(BF16)
        for i, slot in enumerate(slots):
            store(slot, product[16 * i : 16 * i + 16])


def pairs_of(slots, partner):
    return [(slot, partner(slot)) for slot in slots if slot < partner(slot)]


def storer(ref):
    def store(slot, value):
        ref[slot] = value

    return store


def loader(ref):
    return lambda slot: ref[slot]


def angle_kernel(low_levels, high_levels, middle, out):
    pieces = [middle[0], middle[1]]
    for ref, n in ((low_levels, 0), (low_levels, 1), (high_levels, 0), (high_levels, 1)):
        pieces += [ref[n, 0], ref[n, 1]]
    pieces += [low_levels[0, 2], low_levels[1, 2], high_levels[0, 2], high_levels[0, 2]]
    stacked = jnp.concatenate([piece.astype(BF16) for piece in pieces], 0)
    perm = permutation(128, lambda rows: (rows & 7) * 16 + (rows >> 3))
    out[...] = dot_last(perm, stacked).astype(BF16)


def source_kernel(
    part, values, phase, phases, leaf, interp, out, coeffs, spare, tables, left, weights, trig, wide
):
    count = 8 * len(part)

    def rows_here(value):
        if len(part) == 2:
            return value
        width = value.shape[1]
        return value.reshape(8, 2, 8, width)[:, part[0]].reshape(64, width)

    pieces = [phases[n, q] for n in (3, 4, 5) for q in (0, 1)]
    pieces += [phases[n, 2] for n in (2, 3, 4, 5)]
    stacked = jnp.concatenate([piece.astype(BF16) for piece in pieces], 0)
    sent = rows_here(dot_last(permutation(128, lambda rows: rows), stacked))
    for e in range(8):
        here = sent[count * e : count * e + count]
        if len(part) == 2:
            for p in range(5):
                out[e, count + p] = here[:, 128 * p : 128 * p + 128].astype(BF16)
        else:
            for p in range(3):
                first = here[:, 256 * p : 256 * p + 128]
                second = here[:, 256 * p + 128 : 256 * p + 256] if p < 2 else first
                out[e, count + p] = jnp.concatenate([first, second], 0).astype(BF16)
    for n in range(3):
        own, other = phases[n, 0], phases[n, 1]
        if n:
            own = own + phases[n - 1, 2]
            other = other + xor_partner(phases[n - 1, 2], 2**n, 1)
        put_trig(rows_here(jnp.transpose(jnp.concatenate([own, other], 0))), tables.at[n])
        put_weights(weights.at[n], [interp[n, 0], interp[n, 1]])
    put_single_trig(phase[...], trig)
    low, high, zeros = halves(leaf[...])
    for n, first, second in ((0, low, zeros), (1, zeros, low), (2, high, zeros), (3, zeros, high)):
        wide[64 * n : 64 * n + 64, 0:128] = first
        wide[64 * n : 64 * n + 64, 128:256] = second
    leaf_pairs = [pair for pair in range(64) if (pair >> 2) & 1 in part]
    place = lambda slot: (slot >> 4) * count + (slot & (count - 1))
    for step in range(0, len(leaf_pairs), 32):
        rows = left.at[(step // 32) % 2]
        chunk = leaf_pairs[step : step + 32]
        for i, pair in enumerate(chunk):
            cosine = trig[pair : pair + 1, 0:128]
            sine = -trig[pair : pair + 1, 128:256]
            for half in range(2):
                block = values[8 * half : 8 * half + 8, 128 * pair : 128 * pair + 128]
                tile = jnp.concatenate([block * cosine, block * sine], 0).astype(BF16)
                rows[16 * i : 16 * i + 16, 128 * half : 128 * half + 128] = tile
        product = jnp.dot(rows[...], wide[...], preferred_element_type=F32).astype(BF16)
        for i, pair in enumerate(chunk):
            coeffs[place(2 * pair)] = product[16 * i : 16 * i + 16, 0:128]
            coeffs[place(2 * pair + 1)] = product[16 * i : 16 * i + 16, 128:256]

    def send(slot, value):
        out[slot // count, slot % count] = value

    slots = range(8 * count)
    for n, load, store in (
        (0, loader(coeffs), storer(spare)),
        (1, loader(spare), storer(coeffs)),
        (2, loader(coeffs), send),
    ):
        pairs = pairs_of(slots, lambda slot: slot ^ 2**n)
        level(pairs, load, lambda slot: slot, tables.at[n], weights.at[n], left, store)


def both(value, half):
    low = lower(value.shape)
    turned = pltpu.roll(value, 64, 1)
    return jnp.where(low, value, turned) if half == 0 else jnp.where(low, turned, value)


def with_partner(value, stride):
    return jnp.where(lower(value.shape), value, xor_partner(value, stride, 0))


def middle_kernel(
    part, received, angles, interp, middle_interp, out, coeffs, spare, tables, left, weights
):
    count = 8 * len(part)
    size = 8 * count
    early = []
    for p in range(5):
        if len(part) == 2:
            tiles = [received[d, count + p].astype(F32) for d in range(8)]
        else:
            at = 8 * (p % 2)
            tiles = [received[d, count + p // 2].astype(F32)[at : at + 8] for d in range(8)]
        early.append(jnp.concatenate(tiles, 0))
    late = lambda p: angles[:, 128 * p : 128 * p + 128].astype(F32)
    pending = both(early[3], 0)
    for j in range(3):
        put_trig(early[j] + with_partner(pending, count * 2**j), tables.at[j])
        put_weights(weights.at[j], [interp[3 + j, 0], interp[3 + j, 1]])
        pending = both(early[3 + (j + 1) // 2], (j + 1) % 2)
    perm = permutation(size, lambda rows: (rows & 7) * count + (rows >> 3))
    pending = jnp.dot(perm, pending.astype(BF16), preferred_element_type=F32)
    put_single_trig(pending + both(late(0), 0), tables.at[3])
    put_weights(weights.at[3], [middle_interp[...]])
    pending = both(late(0), 1)
    for j in range(len(part) + 2):
        put_trig(late(1 + j) + with_partner(pending, 8 * 2**j), tables.at[4 + j])
        put_weights(weights.at[4 + j], [interp[6 + j, 0], interp[6 + j, 1]])
        if j < 3:
            pending = both(late(5 + j // 2), j % 2)

    def arrived(slot):
        return received[slot & 7, slot >> 3]

    def turned_row(slot):
        return (slot & 7) * count + (slot >> 3)

    slots = range(size)
    stores = [storer(coeffs), storer(spare)]
    loads = [loader(coeffs), loader(spare)]
    for j in range(3):
        level(
            pairs_of(slots, lambda slot: slot ^ 2**j),
            arrived if j == 0 else loads[(j + 1) % 2],
            turned_row,
            tables.at[j],
            weights.at[j],
            left,
            stores[j % 2],
        )
    for step in range(0, size, 32):
        rows = left.at[(step // 32) % 2]
        for i in range(32):
            tile = split(coeffs[step + i])
            rows[16 * i : 16 * i + 16, 0:128] = turn(tables.at[3], step + i, 0, tile)
        product = jnp.dot(
            rows[:, 0:128], weights[3, 0:128, :], preferred_element_type=F32
        ).astype(BF16)
        for i in range(32):
            spare[step + i] = product[16 * i : 16 * i + 16]
    last = len(part) + 1
    for j in range(last + 1):
        level(
            pairs_of(slots, lambda slot: slot ^ 8 * 2**j),
            loads[(j + 1) % 2],
            lambda slot: slot,
            tables.at[4 + j],
            weights.at[4 + j],
            left,
            storer(out) if j == last else stores[j % 2],
        )


def join_kernel(first, second, angles, interp, *rest):
    outs = rest[: len(D_PARTS)]
    tables, left, weights = rest[len(D_PARTS) :]
    pending = both(angles[:, 768:896].astype(F32), 0)
    theta = angles[:, 512:640].astype(F32) + with_partner(pending, 64)
    put_trig(theta, tables)
    put_weights(weights, [interp[9, 0], interp[9, 1]])
    for part, out in zip(D_PARTS, outs):
        each = 4 * len(part)

        def load(slot):
            return first[slot] if slot < 64 else second[slot - 64]

        def send(slot, value):
            out[slot >> 3, slot & (each - 1)] = value

        slots = [slot for slot in range(128) if (slot >> 2) & 1 in part]
        pairs = pairs_of(slots, lambda slot: slot ^ 64)
        level(pairs, load, lambda slot: slot, tables, weights, left, send)


def target_kernel(
    part, received, before, phases10, phases11, phases12, final, interp, final_interp, phase, *rest
):
    out, coeffs, spare, tables, left, weights, trig, wide = rest[-8:]
    each = 4 * len(part)
    size = 16 * each
    first_row = 64 * part[0]

    def rows_here(value):
        return value[first_row : first_row + size]

    pending = before[0, 2]
    for j, ref in enumerate((phases10, phases11, phases12)):
        own = ref[0, 0] + pending
        other = ref[0, 1] + xor_partner(pending, 2**j, 1)
        put_trig(rows_here(jnp.transpose(jnp.concatenate([own, other], 0))), tables.at[j])
        put_weights(weights.at[j], [interp[10 + j, 0], interp[10 + j, 1]])
        pending = ref[0, 2]
    pending = final[...] + pending
    put_single_trig(
        rows_here(jnp.transpose(jnp.concatenate([pending, pending], 0))), tables.at[3]
    )
    put_single_trig(phase[...], trig)
    low, high, zeros = halves(final_interp[...])
    for n, first, second in ((0, low, zeros), (1, zeros, low), (2, high, zeros), (3, zeros, high)):
        wide[64 * n : 64 * n + 64, 0:128] = first
        wide[64 * n : 64 * n + 64, 128:256] = second
    slots = range(size)
    for j, load, store in (
        (0, lambda slot: received[slot & 15, slot >> 4], storer(coeffs)),
        (1, loader(coeffs), storer(spare)),
        (2, loader(spare), storer(coeffs)),
    ):
        pairs = pairs_of(slots, lambda slot: slot ^ 2**j)
        level(pairs, load, lambda slot: slot, tables.at[j], weights.at[j], left, store)
    for step in range(0, size // 2, 32):
        rows = left.at[(step // 32) % 2]
        for i in range(32):
            for odd in range(2):
                slot = 2 * (step + i) + odd
                tile = turn(tables.at[3], slot, 0, split(coeffs[slot]))
                rows[16 * i : 16 * i + 16, 128 * odd : 128 * odd + 128] = tile
        product = jnp.dot(rows[...], wide[...], preferred_element_type=F32)
        for i in range(32):
            pair = step + i
            row = 32 * part[0] + pair
            cosine = trig[row : row + 1, 0:128]
            sine = trig[row : row + 1, 128:256]
            for half in range(2):
                real = product[16 * i : 16 * i + 8, 128 * half : 128 * half + 128]
                imag = product[16 * i + 8 : 16 * i + 16, 128 * half : 128 * half + 128]
                inputs = slice(8 * half, 8 * half + 8)
                points = slice(128 * pair, 128 * pair + 128)
                out[0, inputs, points] = real * cosine - imag * sine
                out[1, inputs, points] = real * sine + imag * cosine


def whole(shape):
    return pl.BlockSpec(shape, lambda i: (0,) * len(shape))


def levels(count, index):
    return pl.BlockSpec((count, 3, 64, 128), lambda i: (index, 0, 0, 0))


def scratch(slots, stages):
    return [
        pltpu.VMEM((slots, 16, 128), BF16),
        pltpu.VMEM((slots, 16, 128), BF16),
        pltpu.VMEM((stages, slots, 512), F32),
        pltpu.VMEM((2, 32 * PAIRS, 256), BF16),
        pltpu.VMEM((stages, 256, 128), BF16),
    ]


def call(kernel, name, in_specs, outs, scratch_shapes, **more):
    many = isinstance(outs, list)
    return pl.pallas_call(
        kernel,
        grid=(1,),
        in_specs=in_specs,
        out_specs=more.pop("out_specs", [whole(o.shape) for o in outs] if many else whole(outs.shape)),
        out_shape=outs,
        scratch_shapes=scratch_shapes,
        compiler_params=pltpu.CompilerParams(vmem_limit_bytes=40 * 1024 * 1024),
        name=name,
        **more,
    )


def shape_of(*shape, dtype=BF16):
    return jax.ShapeDtypeStruct(shape, dtype)


def shards(
    source_values,
    source_phase,
    leaf_interp,
    level_interp,
    level_phase,
    middle_interp,
    middle_phase,
    final_phase,
    final_interp,
    target_phase,
):
    phases = jnp.swapaxes(level_phase, 2, 3)
    middle = jnp.swapaxes(middle_phase, 1, 2)
    final = jnp.swapaxes(final_phase, 0, 1)
    interp_spec = whole((13, 2, 64, 64))
    matrix = whole((64, 64))
    angles = call(
        angle_kernel,
        "angles",
        [levels(2, 3), levels(2, 4), whole((2, 64, 128))],
        shape_of(128, 896),
        [],
    )(phases, phases, middle)
    angles = lax.all_to_all(
        angles.reshape(16, 8, 896), "tgt", split_axis=0, concat_axis=0, tiled=True
    ).reshape(128, 896)
    joined = []
    for part in E_PARTS:
        count = 8 * len(part)
        blocks = count + (5 if len(part) == 2 else 3)
        sent = call(
            functools.partial(source_kernel, part),
            "source_side",
            [whole((16, 8192)), whole((64, 128)), levels(6, 0), matrix, interp_spec],
            shape_of(8, blocks, 16, 128),
            scratch(8 * count, 3) + [pltpu.VMEM((64, 256), F32), pltpu.VMEM((256, 256), BF16)],
        )(source_values, source_phase.reshape(64, 128), phases, leaf_interp, level_interp)
        received = lax.all_to_all(sent, "src", split_axis=0, concat_axis=0, tiled=True)
        rows = pl.BlockSpec((8 * count, 896), lambda i, at=part[0]: (at, 0))
        joined.append(
            call(
                functools.partial(middle_kernel, part),
                "middle",
                [whole((8, blocks, 16, 128)), rows, interp_spec, matrix],
                shape_of(8 * count, 16, 128),
                scratch(8 * count, 8),
            )(received, angles, level_interp, middle_interp)
        )
    if len(E_PARTS) == 2:
        sent = call(
            join_kernel,
            "join",
            [whole((64, 16, 128)), whole((64, 16, 128)), whole((128, 896)), interp_spec],
            [shape_of(16, 4 * len(part), 16, 128) for part in D_PARTS],
            [
                pltpu.VMEM((128, 512), F32),
                pltpu.VMEM((2, 32 * PAIRS, 256), BF16),
                pltpu.VMEM((256, 128), BF16),
            ],
        )(*joined, angles, level_interp)
    else:
        sent = [joined[0].reshape(16, 8, 16, 128)]
    out = None
    for part, piece in zip(D_PARTS, sent):
        received = lax.all_to_all(piece, "tgt", split_axis=0, concat_axis=0, tiled=True)
        operands = [received, phases, phases, phases, phases, final, level_interp, final_interp]
        operands.append(target_phase.reshape(64, 128))
        specs = [whole(received.shape)] + [levels(1, n) for n in (9, 10, 11, 12)]
        specs += [whole((64, 128)), interp_spec, matrix, whole((64, 128))]
        more = {}
        if out is not None:
            operands.append(out)
            specs.append(pl.BlockSpec(memory_space=pl.ANY))
            more["input_output_aliases"] = {len(operands) - 1: 0}
        out = call(
            functools.partial(target_kernel, part),
            "target_side",
            specs,
            shape_of(2, 16, 8192, dtype=F32),
            scratch(64 * len(part), 4)
            + [pltpu.VMEM((64, 256), F32), pltpu.VMEM((256, 256), BF16)],
            out_specs=pl.BlockSpec(
                (2, 16, 4096 * len(part)), lambda i, at=part[0]: (0, 0, at)
            ),
            **more,
        )(*operands)
    return out


def solution(mesh):
    return jax.shard_map(
        shards,
        mesh=mesh,
        in_specs=(
            P(None, ("src", "tgt")),
            P(("src", "tgt")),
            P(),
            P(),
            P(None, None, ("src", "tgt"), None),
            P(),
            P(None, ("src", "tgt"), None),
            P(("src", "tgt"), None),
            P(),
            P(("src", "tgt")),
        ),
        out_specs=P(None, None, ("src", "tgt")),
        check_vma=False,
    )
```

profile of v0, /device:TPU:1, one launch (start us, length us, event | category | flops | bytes accessed | tf_op | source)
XLA Modules:
  0.0 59.7 jit_solution(3360752620957187575)
XLA Ops:
  0.0 0.0 copy-start
  0.0 1.3 %copy-done = f32[13,3,128,64]{2,3,1,0:T(8,128)S(1)} copy-done((f32[13,3,128,64]{2,3,1,0:T(8,128)S(1)}, f32[13,3,128,64]{2,3,1,0:T(8,128)}, u32[]{:S(2)}) %copy-start) | copy-done | bytes 1277976
  1.3 0.0 copy-start.4
  1.3 0.8 %copy-done.4 = f32[2,128,64]{1,2,0:T(8,128)S(1)} copy-done((f32[2,128,64]{1,2,0:T(8,128)S(1)}, f32[2,128,64]{1,2,0:T(8,128)}, u32[]{:S(2)}) %copy-start.4) | copy-done | bytes 65560
  2.1 0.0 copy-start.1
  2.2 0.0 copy-start.8
  2.2 0.9 %angles.1 = bf16[128,896]{1,0:T(8,128)(2,1)} custom-call(f32[13,3,64,128]{3,2,1,0:T(8,128)S(1)} %bitcast.8, f32[13,3,64,128]{3,2,1,0:T(8,128)S(1)} %bitcast.9, f32[2,64,128]{2,1,0:T(8,128)S(1)} %bitcast.17), custom_call_target="tpu_custom_call" | custom-call | tf_op jit(solution)/shard_map/angles/pallas_call | solution.py:431
  3.1 9.1 %all-to-all-start.1 = ((bf16[16,8,896]{2,1,0:T(8,128)(2,1)}), bf16[16,8,896]{2,1,0:T(8,128)(2,1)S(1)}, u32[]{:S(2)}, u32[]{:S(2)}) async-start(bf16[16,8,896]{2,1,0:T(8,128)(2,1)} %bitcast.3), calls=%async_computation.1 | async-start | bytes 458752 | tf_op jit(solution)/shard_map/all_to_all | solution.py:438
  12.2 0.0 copy-done.1
  12.2 0.0 copy-done.2
  12.2 0.0 copy-done.3
  12.2 0.0 copy-done.5
  12.3 0.0 copy-done.8
  12.3 1.9 %source_side.1 = bf16[8,21,16,128]{3,2,1,0:T(8,128)(2,1)S(1)} custom-call(f32[16,8192]{1,0:T(8,128)S(1)} %copy-done.3, f32[64,128]{1,0:T(8,128)S(1)} %bitcast.18, f32[13,3,64,128]{3,2,1,0:T(8,128)S(1)} %bitcast.10, bf16[64,64]{1,0:T(8,128)(2,1)S(1)} %copy-done.8, bf16[13,2,64,64]{3,2,1,0:T(8,128)(2,1)S(1)} %copy-done.2), custom_call_target="tpu_custom_call" | custom-call | tf_op jit(solution)/shard_map/source_side/pallas_call | solution.py:445
  14.1 0.0 copy-start.9
  14.1 6.7 %all-to-all-done.1 = bf16[16,8,896]{2,1,0:T(8,128)(2,1)S(1)} async-done(((bf16[16,8,896]{2,1,0:T(8,128)(2,1)}), bf16[16,8,896]{2,1,0:T(8,128)(2,1)S(1)}, u32[]{:S(2)}, u32[]{:S(2)}) %all-to-all-start.1) | async-done | bytes 229408 | tf_op jit(solution)/shard_map/all_to_all | solution.py:438
  20.8 15.9 %all_to_all.15.received = bf16[8,21,16,128]{3,2,1,0:T(8,128)(2,1)S(1)} all-to-all(bf16[8,21,16,128]{3,2,1,0:T(8,128)(2,1)S(1)} %source_side.1), channel_id=1, replica_groups=mesh['src'=8,'tgt'=16] {'src'}, dimensions={0} | all-to-all | bytes 1376256 | tf_op jit(solution)/shard_map/all_to_all | solution.py:452
  36.8 0.0 copy-done.9
  36.8 4.2 %middle.1 = bf16[128,16,128]{2,1,0:T(8,128)(2,1)S(1)} custom-call(bf16[8,21,16,128]{3,2,1,0:T(8,128)(2,1)S(1)} %all_to_all.15.received, bf16[128,896]{1,0:T(8,128)(2,1)S(1)} %bitcast.16, bf16[13,2,64,64]{3,2,1,0:T(8,128)(2,1)S(1)} %copy-done.2, bf16[64,64]{1,0:T(8,128)(2,1)S(1)} %copy-done.9), custom_call_target="tpu_custom_call" | custom-call | tf_op jit(solution)/shard_map/middle/pallas_call | solution.py:455
  41.0 15.6 %all_to_all.16.received = bf16[16,8,16,128]{3,2,1,0:T(8,128)(2,1)S(1)} all-to-all(bf16[16,8,16,128]{3,2,1,0:T(8,128)(2,1)S(1)} %bitcast.15), channel_id=1, replica_groups=mesh['src'=8,'tgt'=16] {'tgt'}, dimensions={0} | all-to-all | bytes 1048576 | tf_op jit(solution)/shard_map/all_to_all | solution.py:479
  56.6 0.0 copy-done.6
  56.6 0.0 copy-done.7
  56.6 0.0 copy-done.10
  56.6 3.1 %target_side.1 = f32[2,16,8192]{2,1,0:T(8,128)} custom-call(bf16[16,8,16,128]{3,2,1,0:T(8,128)(2,1)S(1)} %all_to_all.16.received, f32[13,3,64,128]{3,2,1,0:T(8,128)S(1)} %bitcast.11, f32[13,3,64,128]{3,2,1,0:T(8,128)S(1)} %bitcast.12, f32[13,3,64,128]{3,2,1,0:T(8,128)S(1)} %bitcast.13, f32[13,3,64,128]{3,2,1,0:T(8,128)S(1)} %bitcast.14, ...), custom_call_target="tpu_custom_call" | custom-call | tf_op jit(solution)/shard_map/target_side/pallas_call | solution.py:489
  (6 shorter events, 0.0 us)
Async XLA Ops:
  0.0 1.3 %copy-start = (f32[13,3,128,64]{2,3,1,0:T(8,128)S(1)}, f32[13,3,128,64]{2,3,1,0:T(8,128)}, u32[]{:S(2)}) copy-start(f32[13,3,128,64]{2,3,1,0:T(8,128)} %param.14) | copy-start | bytes 3833860
  1.3 0.8 %copy-start.4 = (f32[2,128,64]{1,2,0:T(8,128)S(1)}, f32[2,128,64]{1,2,0:T(8,128)}, u32[]{:S(2)}) copy-start(f32[2,128,64]{1,2,0:T(8,128)} %param.16) | copy-start | bytes 196612
  2.1 10.1 %copy-start.1 = (f32[13,3,128,64]{2,3,1,0:T(8,128)S(1)}, f32[13,3,128,64]{2,3,1,0:T(8,128)}, u32[]{:S(2)}) copy-start(f32[13,3,128,64]{2,3,1,0:T(8,128)} %param.14) | copy-start | bytes 3833860
  2.1 10.1 %copy-start.2 = (bf16[13,2,64,64]{3,2,1,0:T(8,128)(2,1)S(1)}, bf16[13,2,64,64]{3,2,1,0:T(8,128)(2,1)}, u32[]{:S(2)}) copy-start(bf16[13,2,64,64]{3,2,1,0:T(8,128)(2,1)} %interp.5) | copy-start | bytes 638980
  2.1 10.1 %copy-start.3 = (f32[16,8192]{1,0:T(8,128)S(1)}, f32[16,8192]{1,0:T(8,128)}, u32[]{:S(2)}) copy-start(f32[16,8192]{1,0:T(8,128)} %values.1) | copy-start | bytes 1572868
  2.2 10.1 %copy-start.5 = (f32[8192]{0:T(1024)S(1)}, f32[8192]{0:T(1024)}, u32[]{:S(2)}) copy-start(f32[8192]{0:T(1024)} %param.11) | copy-start | bytes 98308
  2.2 10.1 %copy-start.8 = (bf16[64,64]{1,0:T(8,128)(2,1)S(1)}, bf16[64,64]{1,0:T(8,128)(2,1)}, u32[]{:S(2)}) copy-start(bf16[64,64]{1,0:T(8,128)(2,1)} %leaf.1) | copy-start | bytes 24580
  3.1 17.7 %all-to-all-start.1 = ((bf16[16,8,896]{2,1,0:T(8,128)(2,1)}), bf16[16,8,896]{2,1,0:T(8,128)(2,1)S(1)}, u32[]{:S(2)}, u32[]{:S(2)}) async-start(bf16[16,8,896]{2,1,0:T(8,128)(2,1)} %bitcast.3), calls=%async_computation.1 | async-start | bytes 458752 | tf_op jit(solution)/shard_map/all_to_all | solution.py:438
  14.1 22.6 %copy-start.9 = (bf16[64,64]{1,0:T(8,128)(2,1)S(1)}, bf16[64,64]{1,0:T(8,128)(2,1)}, u32[]{:S(2)}) copy-start(bf16[64,64]{1,0:T(8,128)(2,1)} %middle_interp.1) | copy-start | bytes 24580
  36.8 19.9 %copy-start.6 = (f32[128,64]{0,1:T(8,128)S(1)}, f32[128,64]{0,1:T(8,128)}, u32[]{:S(2)}) copy-start(f32[128,64]{0,1:T(8,128)} %param.17) | copy-start | bytes 98308
  36.8 19.9 %copy-start.7 = (f32[8192]{0:T(1024)S(1)}, f32[8192]{0:T(1024)}, u32[]{:S(2)}) copy-start(f32[8192]{0:T(1024)} %param.19) | copy-start | bytes 98308
  36.8 19.9 %copy-start.10 = (bf16[64,64]{1,0:T(8,128)(2,1)S(1)}, bf16[64,64]{1,0:T(8,128)(2,1)}, u32[]{:S(2)}) copy-start(bf16[64,64]{1,0:T(8,128)(2,1)} %final_interp.1) | copy-start | bytes 24580
where the time goes:
time: 60.1 us; the launch traced here: 59.7 us
  blocking collectives  31.5 us (52%)
  Pallas kernels  10.1 us (17%)
  starting transfers between devices  9.13 us (15%)
  waiting for transfers between devices  6.67 us (11%)
  local copies, waits for them, and re-layouts  2.18 us (4%)
    all_to_all x1, blocking collectives, shards(): lax.all_to_all(sent, 'src', split_axis=0, concat_axis=0, tiled=True)  15.9 us
    all_to_all x1, blocking collectives, shards(): lax.all_to_all(piece, 'tgt', split_axis=0, concat_axis=0, tiled=True)  15.6 us
    all_to_all x1, starting transfers between devices, shards(): lax.all_to_all(angles.reshape(16, 8, 896), 'tgt', split_axis=0, concat_ax...  9.13 us
    all_to_all x1, waiting for transfers between devices, shards(): lax.all_to_all(angles.reshape(16, 8, 896), 'tgt', split_axis=0, concat_ax...  6.67 us
    pallas_call x1, Pallas kernels, shards(): call(functools.partial(middle_kernel, part), 'middle', [whole((8, blocks,...  4.24 us
    pallas_call x1, Pallas kernels, shards(): call(functools.partial(target_kernel, part), 'target_side', specs, shape_...  3.09 us
    unnamed x22, local copies, waits for them, and re-layouts  2.18 us
    pallas_call x1, Pallas kernels, shards(): call(functools.partial(source_kernel, part), 'source_side', [whole((16, 8...  1.87 us
  transfers between devices with their start and end apart: 1, of which 1 were waited for; matrix products, arithmetic and copies ran while one was open for 0% of the time, Pallas kernels for 3%

commit v1 on v0

--- a/solution.py
+++ b/solution.py
@@ -11,9 +11,7 @@
 
 F32 = jnp.float32
 BF16 = jnp.bfloat16
-PAIRS = 16
-E_PARTS = ((0, 1),)
-D_PARTS = ((0, 1),)
+PAIRS = 32
 SIN_FIT = (3.14159258, -5.16770688, 2.55003138, -0.59804517, 0.07722012)
 COS_FIT = (0.99999995, -4.93479286, 4.05841191, -1.33188014, 0.21969675)
 
@@ -138,18 +136,21 @@
 
 
 def angle_kernel(low_levels, high_levels, middle, out):
+    me = lax.axis_index("src")
     pieces = [middle[0], middle[1]]
     for ref, n in ((low_levels, 0), (low_levels, 1), (high_levels, 0), (high_levels, 1)):
         pieces += [ref[n, 0], ref[n, 1]]
     pieces += [low_levels[0, 2], low_levels[1, 2], high_levels[0, 2], high_levels[0, 2]]
     stacked = jnp.concatenate([piece.astype(BF16) for piece in pieces], 0)
-    perm = permutation(128, lambda rows: (rows & 7) * 16 + (rows >> 3))
+    perm = permutation(128, lambda rows: ((rows & 7) ^ me) * 16 + (rows >> 3))
     out[...] = dot_last(perm, stacked).astype(BF16)
 
 
 def source_kernel(
-    part, values, phase, phases, leaf, interp, out, coeffs, spare, tables, left, weights, trig, wide
+    part, values, phase, phases, leaf, interp, *rest
 ):
+    outs = rest[:8]
+    out, coeffs, spare, tables, left, weights, trig, wide = rest[8:]
     count = 8 * len(part)
 
     def rows_here(value):
@@ -196,7 +197,7 @@
                 block = values[8 * half : 8 * half + 8, 128 * pair : 128 * pair + 128]
                 tile = jnp.concatenate([block * cosine, block * sine], 0).astype(BF16)
                 rows[16 * i : 16 * i + 16, 128 * half : 128 * half + 128] = tile
-        product = jnp.dot(rows[...], wide[...], preferred_element_type=F32).astype(BF16)
+        product = jnp.dot(rows[:512, :], wide[...], preferred_element_type=F32).astype(BF16)
         for i, pair in enumerate(chunk):
             coeffs[place(2 * pair)] = product[16 * i : 16 * i + 16, 0:128]
             coeffs[place(2 * pair + 1)] = product[16 * i : 16 * i + 16, 128:256]
@@ -212,6 +213,9 @@
     ):
         pairs = pairs_of(slots, lambda slot: slot ^ 2**n)
         level(pairs, load, lambda slot: slot, tables.at[n], weights.at[n], left, store)
+    me = lax.axis_index("src")
+    for k in range(8):
+        outs[k][...] = out[me ^ k]
 
 
 def both(value, half):
@@ -224,38 +228,46 @@
     return jnp.where(lower(value.shape), value, xor_partner(value, stride, 0))
 
 
+def late_table_kernel(angles, interp, middle_interp, tables, weights):
+    late = lambda p: angles[:, 128 * p : 128 * p + 128].astype(F32)
+    pending = both(late(0), 1)
+    for j in range(4):
+        put_trig(late(1 + j) + with_partner(pending, 8 * 2**j), tables.at[j])
+        if j < 3:
+            pending = both(late(5 + j // 2), j % 2)
+    for j in range(3):
+        put_weights(weights.at[j], [interp[3 + j, 0], interp[3 + j, 1]])
+    put_weights(weights.at[3], [middle_interp[...], middle_interp[...]])
+    for j in range(4):
+        put_weights(weights.at[4 + j], [interp[6 + j, 0], interp[6 + j, 1]])
+
+
 def middle_kernel(
-    part, received, angles, interp, middle_interp, out, coeffs, spare, tables, left, weights
+    part, *refs
 ):
+    received = refs[:8]
+    angles, late_tables, weights, out, coeffs, spare, tables, left = refs[8:]
     count = 8 * len(part)
     size = 8 * count
     early = []
     for p in range(5):
         if len(part) == 2:
-            tiles = [received[d, count + p].astype(F32) for d in range(8)]
+            tiles = [received[d][count + p].astype(F32) for d in range(8)]
         else:
             at = 8 * (p % 2)
-            tiles = [received[d, count + p // 2].astype(F32)[at : at + 8] for d in range(8)]
+            tiles = [received[d][count + p // 2].astype(F32)[at : at + 8] for d in range(8)]
         early.append(jnp.concatenate(tiles, 0))
     late = lambda p: angles[:, 128 * p : 128 * p + 128].astype(F32)
     pending = both(early[3], 0)
     for j in range(3):
         put_trig(early[j] + with_partner(pending, count * 2**j), tables.at[j])
-        put_weights(weights.at[j], [interp[3 + j, 0], interp[3 + j, 1]])
         pending = both(early[3 + (j + 1) // 2], (j + 1) % 2)
     perm = permutation(size, lambda rows: (rows & 7) * count + (rows >> 3))
     pending = jnp.dot(perm, pending.astype(BF16), preferred_element_type=F32)
     put_single_trig(pending + both(late(0), 0), tables.at[3])
-    put_weights(weights.at[3], [middle_interp[...]])
-    pending = both(late(0), 1)
-    for j in range(len(part) + 2):
-        put_trig(late(1 + j) + with_partner(pending, 8 * 2**j), tables.at[4 + j])
-        put_weights(weights.at[4 + j], [interp[6 + j, 0], interp[6 + j, 1]])
-        if j < 3:
-            pending = both(late(5 + j // 2), j % 2)
 
     def arrived(slot):
-        return received[slot & 7, slot >> 3]
+        return received[slot & 7][slot >> 3]
 
     def turned_row(slot):
         return (slot & 7) * count + (slot >> 3)
@@ -279,7 +291,7 @@
             tile = split(coeffs[step + i])
             rows[16 * i : 16 * i + 16, 0:128] = turn(tables.at[3], step + i, 0, tile)
         product = jnp.dot(
-            rows[:, 0:128], weights[3, 0:128, :], preferred_element_type=F32
+            rows[:512, 0:128], weights[3, 0:128, :], preferred_element_type=F32
         ).astype(BF16)
         for i in range(32):
             spare[step + i] = product[16 * i : 16 * i + 16]
@@ -289,80 +301,55 @@
             pairs_of(slots, lambda slot: slot ^ 8 * 2**j),
             loads[(j + 1) % 2],
             lambda slot: slot,
-            tables.at[4 + j],
+            late_tables.at[j],
             weights.at[4 + j],
             left,
             storer(out) if j == last else stores[j % 2],
         )
 
 
-def join_kernel(first, second, angles, interp, *rest):
-    outs = rest[: len(D_PARTS)]
-    tables, left, weights = rest[len(D_PARTS) :]
-    pending = both(angles[:, 768:896].astype(F32), 0)
-    theta = angles[:, 512:640].astype(F32) + with_partner(pending, 64)
-    put_trig(theta, tables)
-    put_weights(weights, [interp[9, 0], interp[9, 1]])
-    for part, out in zip(D_PARTS, outs):
-        each = 4 * len(part)
-
-        def load(slot):
-            return first[slot] if slot < 64 else second[slot - 64]
-
-        def send(slot, value):
-            out[slot >> 3, slot & (each - 1)] = value
-
-        slots = [slot for slot in range(128) if (slot >> 2) & 1 in part]
-        pairs = pairs_of(slots, lambda slot: slot ^ 64)
-        level(pairs, load, lambda slot: slot, tables, weights, left, send)
+def target_table_kernel(phases, final, interp, phase, tables, weights, trig):
+    pending = phases[9, 2]
+    for j in range(3):
+        own = phases[10 + j, 0] + pending
+        other = phases[10 + j, 1] + xor_partner(pending, 2**j, 1)
+        put_trig(jnp.transpose(jnp.concatenate([own, other], 0)), tables.at[j])
+        put_weights(weights.at[j], [interp[10 + j, 0], interp[10 + j, 1]])
+        pending = phases[10 + j, 2]
+    pending = final[...] + pending
+    put_single_trig(jnp.transpose(jnp.concatenate([pending, pending], 0)), tables.at[3])
+    put_single_trig(phase[...], trig)
 
 
 def target_kernel(
-    part, received, before, phases10, phases11, phases12, final, interp, final_interp, phase, *rest
+    received, tables, weights, trig, final_interp, result, coeffs, spare, left, wide, out, sems
 ):
-    out, coeffs, spare, tables, left, weights, trig, wide = rest[-8:]
-    each = 4 * len(part)
-    size = 16 * each
-    first_row = 64 * part[0]
-
-    def rows_here(value):
-        return value[first_row : first_row + size]
-
-    pending = before[0, 2]
-    for j, ref in enumerate((phases10, phases11, phases12)):
-        own = ref[0, 0] + pending
-        other = ref[0, 1] + xor_partner(pending, 2**j, 1)
-        put_trig(rows_here(jnp.transpose(jnp.concatenate([own, other], 0))), tables.at[j])
-        put_weights(weights.at[j], [interp[10 + j, 0], interp[10 + j, 1]])
-        pending = ref[0, 2]
-    pending = final[...] + pending
-    put_single_trig(
-        rows_here(jnp.transpose(jnp.concatenate([pending, pending], 0))), tables.at[3]
-    )
-    put_single_trig(phase[...], trig)
+    me = lax.axis_index("src")
     low, high, zeros = halves(final_interp[...])
     for n, first, second in ((0, low, zeros), (1, zeros, low), (2, high, zeros), (3, zeros, high)):
         wide[64 * n : 64 * n + 64, 0:128] = first
         wide[64 * n : 64 * n + 64, 128:256] = second
+    size = 128
+    copies = []
     slots = range(size)
     for j, load, store in (
-        (0, lambda slot: received[slot & 15, slot >> 4], storer(coeffs)),
+        (0, lambda slot: received[slot & 15, (slot >> 4) ^ me], storer(coeffs)),
         (1, loader(coeffs), storer(spare)),
         (2, loader(spare), storer(coeffs)),
     ):
         pairs = pairs_of(slots, lambda slot: slot ^ 2**j)
         level(pairs, load, lambda slot: slot, tables.at[j], weights.at[j], left, store)
-    for step in range(0, size // 2, 32):
-        rows = left.at[(step // 32) % 2]
-        for i in range(32):
+    for step in range(0, size // 2, 16):
+        rows = left.at[(step // 16) % 2]
+        for i in range(16):
             for odd in range(2):
                 slot = 2 * (step + i) + odd
                 tile = turn(tables.at[3], slot, 0, split(coeffs[slot]))
                 rows[16 * i : 16 * i + 16, 128 * odd : 128 * odd + 128] = tile
-        product = jnp.dot(rows[...], wide[...], preferred_element_type=F32)
-        for i in range(32):
+        product = jnp.dot(rows[:256, :], wide[...], preferred_element_type=F32)
+        for i in range(16):
             pair = step + i
-            row = 32 * part[0] + pair
+            row = pair
             cosine = trig[row : row + 1, 0:128]
             sine = trig[row : row + 1, 128:256]
             for half in range(2):
@@ -372,36 +359,34 @@
                 points = slice(128 * pair, 128 * pair + 128)
                 out[0, inputs, points] = real * cosine - imag * sine
                 out[1, inputs, points] = real * sine + imag * cosine
-
-
-def whole(shape):
-    return pl.BlockSpec(shape, lambda i: (0,) * len(shape))
+        points = slice(128 * step, 128 * step + 2048)
+        copies.append(
+            pltpu.make_async_copy(
+                out.at[:, :, points], result.at[:, :, points], sems.at[step // 16]
+            )
+        )
+        copies[-1].start()
+    for copy in copies:
+        copy.wait()
+
+
+def whole(_):
+    return pl.BlockSpec(memory_space=pltpu.VMEM)
 
 
 def levels(count, index):
     return pl.BlockSpec((count, 3, 64, 128), lambda i: (index, 0, 0, 0))
-
-
-def scratch(slots, stages):
-    return [
-        pltpu.VMEM((slots, 16, 128), BF16),
-        pltpu.VMEM((slots, 16, 128), BF16),
-        pltpu.VMEM((stages, slots, 512), F32),
-        pltpu.VMEM((2, 32 * PAIRS, 256), BF16),
-        pltpu.VMEM((stages, 256, 128), BF16),
-    ]
 
 
 def call(kernel, name, in_specs, outs, scratch_shapes, **more):
     many = isinstance(outs, list)
     return pl.pallas_call(
         kernel,
-        grid=(1,),
         in_specs=in_specs,
         out_specs=more.pop("out_specs", [whole(o.shape) for o in outs] if many else whole(outs.shape)),
         out_shape=outs,
         scratch_shapes=scratch_shapes,
-        compiler_params=pltpu.CompilerParams(vmem_limit_bytes=40 * 1024 * 1024),
+        compiler_params=pltpu.CompilerParams(vmem_limit_bytes=more.pop("room", 24) * 1024 * 1024),
         name=name,
         **more,
     )
@@ -431,74 +416,69 @@
     angles = call(
         angle_kernel,
         "angles",
-        [levels(2, 3), levels(2, 4), whole((2, 64, 128))],
+        [levels(2, 3), levels(2, 4), pl.BlockSpec((2, 64, 128), lambda i: (0, 0, 0))],
         shape_of(128, 896),
         [],
+        grid=(1,),
+        out_specs=pl.BlockSpec((128, 896), lambda i: (0, 0)),
+        room=60,
     )(phases, phases, middle)
     angles = lax.all_to_all(
         angles.reshape(16, 8, 896), "tgt", split_axis=0, concat_axis=0, tiled=True
     ).reshape(128, 896)
-    joined = []
-    for part in E_PARTS:
-        count = 8 * len(part)
-        blocks = count + (5 if len(part) == 2 else 3)
-        sent = call(
-            functools.partial(source_kernel, part),
-            "source_side",
-            [whole((16, 8192)), whole((64, 128)), levels(6, 0), matrix, interp_spec],
-            shape_of(8, blocks, 16, 128),
-            scratch(8 * count, 3) + [pltpu.VMEM((64, 256), F32), pltpu.VMEM((256, 256), BF16)],
-        )(source_values, source_phase.reshape(64, 128), phases, leaf_interp, level_interp)
-        received = lax.all_to_all(sent, "src", split_axis=0, concat_axis=0, tiled=True)
-        rows = pl.BlockSpec((8 * count, 896), lambda i, at=part[0]: (at, 0))
-        joined.append(
-            call(
-                functools.partial(middle_kernel, part),
-                "middle",
-                [whole((8, blocks, 16, 128)), rows, interp_spec, matrix],
-                shape_of(8 * count, 16, 128),
-                scratch(8 * count, 8),
-            )(received, angles, level_interp, middle_interp)
-        )
-    if len(E_PARTS) == 2:
-        sent = call(
-            join_kernel,
-            "join",
-            [whole((64, 16, 128)), whole((64, 16, 128)), whole((128, 896)), interp_spec],
-            [shape_of(16, 4 * len(part), 16, 128) for part in D_PARTS],
-            [
-                pltpu.VMEM((128, 512), F32),
-                pltpu.VMEM((2, 32 * PAIRS, 256), BF16),
-                pltpu.VMEM((256, 128), BF16),
-            ],
-        )(*joined, angles, level_interp)
-    else:
-        sent = [joined[0].reshape(16, 8, 16, 128)]
-    out = None
-    for part, piece in zip(D_PARTS, sent):
-        received = lax.all_to_all(piece, "tgt", split_axis=0, concat_axis=0, tiled=True)
-        operands = [received, phases, phases, phases, phases, final, level_interp, final_interp]
-        operands.append(target_phase.reshape(64, 128))
-        specs = [whole(received.shape)] + [levels(1, n) for n in (9, 10, 11, 12)]
-        specs += [whole((64, 128)), interp_spec, matrix, whole((64, 128))]
-        more = {}
-        if out is not None:
-            operands.append(out)
-            specs.append(pl.BlockSpec(memory_space=pl.ANY))
-            more["input_output_aliases"] = {len(operands) - 1: 0}
-        out = call(
-            functools.partial(target_kernel, part),
-            "target_side",
-            specs,
-            shape_of(2, 16, 8192, dtype=F32),
-            scratch(64 * len(part), 4)
-            + [pltpu.VMEM((64, 256), F32), pltpu.VMEM((256, 256), BF16)],
-            out_specs=pl.BlockSpec(
-                (2, 16, 4096 * len(part)), lambda i, at=part[0]: (0, 0, at)
-            ),
-            **more,
-        )(*operands)
-    return out
+    late_tables, weights = call(
+        late_table_kernel,
+        "late_tables",
+        [whole(None)] * 3,
+        [shape_of(4, 128, 512, dtype=F32), shape_of(8, 256, 128)],
+        [],
+    )(angles, level_interp, middle_interp)
+    target_tables = call(
+        target_table_kernel,
+        "target_tables",
+        [whole(None)] * 4,
+        [
+            shape_of(4, 128, 512, dtype=F32),
+            shape_of(3, 256, 128),
+            shape_of(64, 256, dtype=F32),
+        ],
+        [],
+    )(phases, final, level_interp, target_phase.reshape(64, 128))
+    tiles = pltpu.VMEM((128, 16, 128), BF16)
+    left = pltpu.VMEM((2, 32 * PAIRS, 256), BF16)
+    part = (0, 1)
+    sent = call(
+        functools.partial(source_kernel, part),
+        "source_side",
+        [whole(None)] * 5,
+        [shape_of(21, 16, 128)] * 8,
+        [pltpu.VMEM((8, 21, 16, 128), BF16), tiles, tiles]
+        + [pltpu.VMEM((3, 128, 512), F32), left, pltpu.VMEM((3, 256, 128), BF16)]
+        + [pltpu.VMEM((64, 256), F32), pltpu.VMEM((256, 256), BF16)],
+    )(source_values, source_phase.reshape(64, 128), phases, leaf_interp, level_interp)
+    received = [
+        lax.ppermute(piece, "src", [(i, i ^ k) for i in range(8)]) if k else piece
+        for k, piece in enumerate(sent)
+    ]
+    sent = call(
+        functools.partial(middle_kernel, part),
+        "middle",
+        [whole(None)] * 11,
+        shape_of(128, 16, 128),
+        [tiles, tiles, pltpu.VMEM((4, 128, 512), F32), left],
+    )(*received, angles, late_tables, weights)
+    received = lax.all_to_all(
+        sent.reshape(16, 8, 16, 128), "tgt", split_axis=0, concat_axis=0, tiled=True
+    )
+    return call(
+        target_kernel,
+        "target_side",
+        [whole(None)] * 5,
+        shape_of(2, 16, 8192, dtype=F32),
+        [tiles, tiles, left, pltpu.VMEM((256, 256), BF16)]
+        + [pltpu.VMEM((2, 16, 8192), F32), pltpu.SemaphoreType.DMA((4,))],
+        out_specs=pl.BlockSpec(memory_space=pl.ANY),
+    )(received, *target_tables, final_interp)
 
 
 def solution(mesh):

time: 60.1 us -> 57.5 us (0.957)
  blocking collectives: 31.5 us -> 0 us
  starting transfers between devices: 9.13 us -> 29.9 us
  waiting for transfers between devices: 6.67 us -> 13.4 us
  Pallas kernels: 10.1 us -> 12.1 us
  local copies, waits for them, and re-layouts: 2.18 us -> 1.54 us
    all_to_all x2 -> x0, blocking collectives: 31.5 us -> none  [the longest x1 15.9 us: shards(): lax.all_to_all(sent, 'src', split_axis=0, concat_axis=0, tiled=True)]
    all_to_all x0 -> x1, starting transfers between devices: none -> 10.7 us  [shards(): lax.all_to_all(sent.reshape(16, 8, 16, 128), 'tgt', split_axis=0, concat_...]
    ppermute x0 -> x7, starting transfers between devices: none -> 9.96 us  [shards(): lax.ppermute(piece, 'src', [(i, i ^ k) for i in range(8)])]
    all_to_all x0 -> x1, waiting for transfers between devices: none -> 8.96 us  [shards(): lax.all_to_all(sent.reshape(16, 8, 16, 128), 'tgt', split_axis=0, concat_...]
    all_to_all x1, waiting for transfers between devices: 6.67 us -> 0.01 us  [shards(): lax.all_to_all(angles.reshape(16, 8, 896), 'tgt', split_axis=0, concat_ax...]
    ppermute x0 -> x7, waiting for transfers between devices: none -> 4.45 us  [shards(): lax.ppermute(piece, 'src', [(i, i ^ k) for i in range(8)])]
    pallas_call x4 -> x6, Pallas kernels: 10.1 us -> 12.1 us  [the longest x1 4.28 us: shards(): call(functools.partial(middle_kernel, part), 'middle', [whole(None)] * 11...]
    unnamed x22 -> x18, local copies, waits for them, and re-layouts: 2.18 us -> 1.54 us
  transfers between devices with their start and end apart: 1 -> 9, of which waited for: 1 -> 4; matrix products, arithmetic and copies ran while one was open for 0% -> 0% of each run, Pallas kernels for 3% -> 6%
where the time goes in v1:
time: 57.5 us; the launch traced here: 57 us
  starting transfers between devices  29.9 us (52%)
  waiting for transfers between devices  13.4 us (23%)
  Pallas kernels  12.1 us (21%)
  local copies, waits for them, and re-layouts  1.54 us (3%)
    all_to_all x1, starting transfers between devices, shards(): lax.all_to_all(sent.reshape(16, 8, 16, 128), 'tgt', split_axis=0, concat_...  10.7 us
    ppermute x7, starting transfers between devices, shards(): lax.ppermute(piece, 'src', [(i, i ^ k) for i in range(8)])  9.96 us
    all_to_all x1, starting transfers between devices, shards(): lax.all_to_all(angles.reshape(16, 8, 896), 'tgt', split_axis=0, concat_ax...  9.26 us
    all_to_all x1, waiting for transfers between devices, shards(): lax.all_to_all(sent.reshape(16, 8, 16, 128), 'tgt', split_axis=0, concat_...  8.96 us
    ppermute x7, waiting for transfers between devices, shards(): lax.ppermute(piece, 'src', [(i, i ^ k) for i in range(8)])  4.45 us
    pallas_call x1, Pallas kernels, shards(): call(functools.partial(middle_kernel, part), 'middle', [whole(None)] * 11...  4.28 us
    pallas_call x1, Pallas kernels, shards(): call(target_kernel, 'target_side', [whole(None)] * 5, shape_of(2, 16, 819...  2.5 us
    pallas_call x1, Pallas kernels, shards(): call(angle_kernel, 'angles', [levels(2, 3), levels(2, 4), pl.BlockSpec((2...  2.1 us
  transfers between devices with their start and end apart: 9, of which 4 were waited for; matrix products, arithmetic and copies ran while one was open for 0% of the time, Pallas kernels for 6%

profile of v1, /device:TPU:1, one launch (start us, length us, event | category | flops | bytes accessed | tf_op | source)
XLA Modules:
  0.0 57.0 jit_solution(7005909696205073282)
XLA Ops:
  0.0 2.1 %angles.1 = bf16[128,896]{1,0:T(8,128)(2,1)} custom-call(f32[13,3,64,128]{3,2,1,0:T(8,128)} %bitcast.8, f32[13,3,64,128]{3,2,1,0:T(8,128)} %bitcast.9, f32[2,64,128]{2,1,0:T(8,128)} %bitcast.18), custom_call_target="tpu_custom_call" | custom-call | tf_op jit(solution)/shard_map/angles/pallas_call | solution.py:416
  2.1 9.3 %all-to-all-start = ((bf16[16,8,896]{2,1,0:T(8,128)(2,1)}), bf16[16,8,896]{2,1,0:T(8,128)(2,1)S(1)}, u32[]{:S(2)}, u32[]{:S(2)}) async-start(bf16[16,8,896]{2,1,0:T(8,128)(2,1)} %bitcast.17), calls=%async_computation | async-start | bytes 458752 | tf_op jit(solution)/shard_map/all_to_all | solution.py:426
  11.4 1.9 %source_side.1 = (bf16[21,16,128]{2,1,0:T(8,128)(2,1)S(1)}, bf16[21,16,128]{2,1,0:T(8,128)(2,1)S(1)}, bf16[21,16,128]{2,1,0:T(8,128)(2,1)S(1)}, bf16[21,16,128]{...) custom-call(f32[16,8192]{1,0:T(8,128)S(1)} %copy-done.2, ...), custom_call_target="tpu_custom_call" | custom-call | tf_op jit(solution)/shard_map/source_side/pallas_call | solution.py:450
  13.3 1.4 %collective-permute-start = (bf16[21,16,128]{2,1,0:T(8,128)(2,1)S(1)}, bf16[21,16,128]{2,1,0:T(8,128)(2,1)S(1)}, u32[]{:S(2)}, u32[]{:S(2)}) collective-permute-start(bf16[21,16,128]{2,1,0:T(8,128)(2,1)S(1)} %get-tuple-element.19), channel_id=1, source_target_pairs={{0,16},{16,0},{32,48},{48,32},{64,80},{80,64},{96,112},{112,96},{1... | collective-permute-start | bytes 258056 | tf_op jit(solution)/shard_map/ppermute | solution.py:460
  14.7 2.6 %collective-permute-start.1 = (bf16[21,16,128]{2,1,0:T(8,128)(2,1)S(1)}, bf16[21,16,128]{2,1,0:T(8,128)(2,1)S(1)}, u32[]{:S(2)}, u32[]{:S(2)}) collective-permute-start(bf16[21,16,128]{2,1,0:T(8,128)(2,1)S(1)} %get-tuple-element.20), channel_id=1, source_target_pairs={{0,32},{16,48},{32,0},{48,16},{64,96},{80,112},{96,64},{112,80},{1... | collective-permute-start | bytes 258056 | tf_op jit(solution)/shard_map/ppermute | solution.py:460
  17.4 0.0 collective-permute-start.2
  17.4 0.7 %collective-permute-start.3 = (bf16[21,16,128]{2,1,0:T(8,128)(2,1)S(1)}, bf16[21,16,128]{2,1,0:T(8,128)(2,1)S(1)}, u32[]{:S(2)}, u32[]{:S(2)}) collective-permute-start(bf16[21,16,128]{2,1,0:T(8,128)(2,1)S(1)} %get-tuple-element.22), channel_id=1, source_target_pairs={{0,64},{16,80},{32,96},{48,112},{64,0},{80,16},{96,32},{112,48},{1... | collective-permute-start | bytes 258056 | tf_op jit(solution)/shard_map/ppermute | solution.py:460
  18.1 0.5 collective-permute-start.4
  18.6 0.0 collective-permute-done.refs_1_
  18.6 4.3 %collective-permute-start.5 = (bf16[21,16,128]{2,1,0:T(8,128)(2,1)S(1)}, bf16[21,16,128]{2,1,0:T(8,128)(2,1)S(1)}, u32[]{:S(2)}, u32[]{:S(2)}) collective-permute-start(bf16[21,16,128]{2,1,0:T(8,128)(2,1)S(1)} %get-tuple-element.24), channel_id=1, source_target_pairs={{0,96},{16,112},{32,64},{48,80},{64,32},{80,48},{96,0},{112,16},{1... | collective-permute-start | bytes 258056 | tf_op jit(solution)/shard_map/ppermute | solution.py:460
  22.9 0.0 collective-permute-done.1.refs_2_
  22.9 0.4 collective-permute-start.6
  23.3 0.0 all-to-all-done
  23.3 0.7 %late_tables.1 = (f32[4,128,512]{2,1,0:T(8,128)S(1)}, bf16[8,256,128]{2,1,0:T(8,128)(2,1)S(1)}) custom-call(bf16[128,896]{1,0:T(8,128)(2,1)S(1)} %bitcast.12, bf16[13,2,64,64]{3,2,1,0:T(8,128)(2,1)S(1)} %copy-done.1, bf16[64,64]{1,0:T(8,128)(2,1)S(1)} %copy-done.8), custom_call_target="tpu_custom_call" | custom-call | tf_op jit(solution)/shard_map/late_tables/pallas_call | solution.py:429
  24.0 0.1 collective-permute-done.2.refs_3_
  24.0 1.7 %collective-permute-done.5.refs_6_ = bf16[21,16,128]{2,1,0:T(8,128)(2,1)S(1)} collective-permute-done((bf16[21,16,128]{2,1,0:T(8,128)(2,1)S(1)}, bf16[21,16,128]{2,1,0:T(8,128)(2,1)S(1)}, u32[]{:S(2)}, u32[]{:S(2)}) %collective-permute-start.5) | collective-permute-done | bytes 86048 | tf_op jit(solution)/shard_map/ppermute | solution.py:460
  25.8 2.6 %collective-permute-done.6.refs_7_ = bf16[21,16,128]{2,1,0:T(8,128)(2,1)S(1)} collective-permute-done((bf16[21,16,128]{2,1,0:T(8,128)(2,1)S(1)}, bf16[21,16,128]{2,1,0:T(8,128)(2,1)S(1)}, u32[]{:S(2)}, u32[]{:S(2)}) %collective-permute-start.6) | collective-permute-done | bytes 86048 | tf_op jit(solution)/shard_map/ppermute | solution.py:460
  28.4 4.3 %middle.1 = bf16[128,16,128]{2,1,0:T(8,128)(2,1)} custom-call(bf16[21,16,128]{2,1,0:T(8,128)(2,1)S(1)} %get-tuple-element.18.refs_0_, bf16[21,16,128]{2,1,0:T(8,128)(2,1)S(1)} %collective-permute-done.refs_1_, bf16[21,16,128]{2,1,0:T(8,128)(2,1)S(1)} %collective-permute-done.1.refs_2_, bf16[21,16,128]{2,1,0:T(8,128)(2,1)S(1)} %collective-permute-done.2.refs_3_, ...), custom_call_target="tpu_custom_call" | custom-call | tf_op jit(solution)/shard_map/middle/pallas_call | solution.py:463
  32.7 10.7 %all-to-all-start.1 = ((bf16[16,8,16,128]{3,2,1,0:T(8,128)(2,1)}), bf16[16,8,16,128]{3,2,1,0:T(8,128)(2,1)S(1)}, u32[]{:S(2)}, u32[]{:S(2)}) async-start(bf16[16,8,16,128]{3,2,1,0:T(8,128)(2,1)} %bitcast.5), calls=%async_computation.1 | async-start | bytes 1048576 | tf_op jit(solution)/shard_map/all_to_all | solution.py:470
  43.4 0.8 %copy-done.4 = f32[128,64]{0,1:T(8,128)S(1)} copy-done((f32[128,64]{0,1:T(8,128)S(1)}, f32[128,64]{0,1:T(8,128)}, u32[]{:S(2)}) %copy-start.4) | copy-done | bytes 32792
  44.1 0.8 %copy-done.5 = f32[8192]{0:T(1024)S(1)} copy-done((f32[8192]{0:T(1024)S(1)}, f32[8192]{0:T(1024)}, u32[]{:S(2)}) %copy-start.5) | copy-done | bytes 32792
  44.9 0.7 %target_tables.1 = (f32[4,128,512]{2,1,0:T(8,128)S(1)}, bf16[3,256,128]{2,1,0:T(8,128)(2,1)S(1)}, f32[64,256]{1,0:T(8,128)S(1)}) custom-call(f32[13,3,64,128]{3,2,1,0:T(8,128)S(1)} %bitcast.11, f32[64,128]{1,0:T(8,128)S(1)} %bitcast.15, bf16[13,2,64,64]{3,2,1,0:T(8,128)(2,1)S(1)} %copy-done.1, f32[64,128]{1,0:T(8,128)S(1)} %bitcast.16), custom_call_target="tpu_custom_call" | custom-call | tf_op jit(solution)/shard_map/target_tables/pallas_call | solution.py:436
  45.5 9.0 %all-to-all-done.1.received = bf16[16,8,16,128]{3,2,1,0:T(8,128)(2,1)S(1)} async-done(((bf16[16,8,16,128]{3,2,1,0:T(8,128)(2,1)}), bf16[16,8,16,128]{3,2,1,0:T(8,128)(2,1)S(1)}, u32[]{:S(2)}, u32[]{:S(2)}) %all-to-all-start.1) | async-done | bytes 524320 | tf_op jit(solution)/shard_map/all_to_all | solution.py:470
  54.5 2.5 %target_side.1 = f32[2,16,8192]{2,1,0:T(8,128)} custom-call(bf16[16,8,16,128]{3,2,1,0:T(8,128)(2,1)S(1)} %all-to-all-done.1.received, f32[4,128,512]{2,1,0:T(8,128)S(1)} %get-tuple-element.28.tables, bf16[3,256,128]{2,1,0:T(8,128)(2,1)S(1)} %get-tuple-element.29.weights, f32[64,256]{1,0:T(8,128)S(1)} %get-tuple-element.30.trig, bf16[64,64]{1,0:T(8,128)(2,1)S(1)} %copy-done.7), custom_call_target="tpu_custom_call" | custom-call | tf_op jit(solution)/shard_map/target_side/pallas_call | solution.py:473
  (18 shorter events, 0.0 us)
Async XLA Ops:
  0.0 11.4 %copy-start = (f32[13,3,128,64]{2,3,1,0:T(8,128)S(1)}, f32[13,3,128,64]{2,3,1,0:T(8,128)}, u32[]{:S(2)}) copy-start(f32[13,3,128,64]{2,3,1,0:T(8,128)} %param.14) | copy-start | bytes 3833860
  0.0 11.4 %copy-start.1 = (bf16[13,2,64,64]{3,2,1,0:T(8,128)(2,1)S(1)}, bf16[13,2,64,64]{3,2,1,0:T(8,128)(2,1)}, u32[]{:S(2)}) copy-start(bf16[13,2,64,64]{3,2,1,0:T(8,128)(2,1)} %interp.5) | copy-start | bytes 638980
  0.0 11.4 %copy-start.2 = (f32[16,8192]{1,0:T(8,128)S(1)}, f32[16,8192]{1,0:T(8,128)}, u32[]{:S(2)}) copy-start(f32[16,8192]{1,0:T(8,128)} %values.1) | copy-start | bytes 1572868
  0.0 11.4 %copy-start.3 = (f32[8192]{0:T(1024)S(1)}, f32[8192]{0:T(1024)}, u32[]{:S(2)}) copy-start(f32[8192]{0:T(1024)} %param.11) | copy-start | bytes 98308
  0.0 11.4 %copy-start.6 = (bf16[64,64]{1,0:T(8,128)(2,1)S(1)}, bf16[64,64]{1,0:T(8,128)(2,1)}, u32[]{:S(2)}) copy-start(bf16[64,64]{1,0:T(8,128)(2,1)} %leaf.1) | copy-start | bytes 24580
  2.1 21.2 %copy-start.8 = (bf16[64,64]{1,0:T(8,128)(2,1)S(1)}, bf16[64,64]{1,0:T(8,128)(2,1)}, u32[]{:S(2)}) copy-start(bf16[64,64]{1,0:T(8,128)(2,1)} %middle_interp.1) | copy-start | bytes 24580
  2.1 21.2 %all-to-all-start = ((bf16[16,8,896]{2,1,0:T(8,128)(2,1)}), bf16[16,8,896]{2,1,0:T(8,128)(2,1)S(1)}, u32[]{:S(2)}, u32[]{:S(2)}) async-start(bf16[16,8,896]{2,1,0:T(8,128)(2,1)} %bitcast.17), calls=%async_computation | async-start | bytes 458752 | tf_op jit(solution)/shard_map/all_to_all | solution.py:426
  13.3 5.2 %collective-permute-start = (bf16[21,16,128]{2,1,0:T(8,128)(2,1)S(1)}, bf16[21,16,128]{2,1,0:T(8,128)(2,1)S(1)}, u32[]{:S(2)}, u32[]{:S(2)}) collective-permute-start(bf16[21,16,128]{2,1,0:T(8,128)(2,1)S(1)} %get-tuple-element.19), channel_id=1, source_target_pairs={{0,16},{16,0},{32,48},{48,32},{64,80},{80,64},{96,112},{112,96},{1... | collective-permute-start | bytes 258056 | tf_op jit(solution)/shard_map/ppermute | solution.py:460
  14.7 8.1 %collective-permute-start.1 = (bf16[21,16,128]{2,1,0:T(8,128)(2,1)S(1)}, bf16[21,16,128]{2,1,0:T(8,128)(2,1)S(1)}, u32[]{:S(2)}, u32[]{:S(2)}) collective-permute-start(bf16[21,16,128]{2,1,0:T(8,128)(2,1)S(1)} %get-tuple-element.20), channel_id=1, source_target_pairs={{0,32},{16,48},{32,0},{48,16},{64,96},{80,112},{96,64},{112,80},{1... | collective-permute-start | bytes 258056 | tf_op jit(solution)/shard_map/ppermute | solution.py:460
  17.4 6.7 %collective-permute-start.2 = (bf16[21,16,128]{2,1,0:T(8,128)(2,1)S(1)}, bf16[21,16,128]{2,1,0:T(8,128)(2,1)S(1)}, u32[]{:S(2)}, u32[]{:S(2)}) collective-permute-start(bf16[21,16,128]{2,1,0:T(8,128)(2,1)S(1)} %get-tuple-element.21), channel_id=1, source_target_pairs={{0,48},{16,32},{32,16},{48,0},{64,112},{80,96},{96,80},{112,64},{1... | collective-permute-start | bytes 258056 | tf_op jit(solution)/shard_map/ppermute | solution.py:460
  17.4 6.7 %collective-permute-start.3 = (bf16[21,16,128]{2,1,0:T(8,128)(2,1)S(1)}, bf16[21,16,128]{2,1,0:T(8,128)(2,1)S(1)}, u32[]{:S(2)}, u32[]{:S(2)}) collective-permute-start(bf16[21,16,128]{2,1,0:T(8,128)(2,1)S(1)} %get-tuple-element.22), channel_id=1, source_target_pairs={{0,64},{16,80},{32,96},{48,112},{64,0},{80,16},{96,32},{112,48},{1... | collective-permute-start | bytes 258056 | tf_op jit(solution)/shard_map/ppermute | solution.py:460
  18.1 5.9 %collective-permute-start.4 = (bf16[21,16,128]{2,1,0:T(8,128)(2,1)S(1)}, bf16[21,16,128]{2,1,0:T(8,128)(2,1)S(1)}, u32[]{:S(2)}, u32[]{:S(2)}) collective-permute-start(bf16[21,16,128]{2,1,0:T(8,128)(2,1)S(1)} %get-tuple-element.23), channel_id=1, source_target_pairs={{0,80},{16,64},{32,112},{48,96},{64,16},{80,0},{96,48},{112,32},{1... | collective-permute-start | bytes 258056 | tf_op jit(solution)/shard_map/ppermute | solution.py:460
  18.6 7.2 %collective-permute-start.5 = (bf16[21,16,128]{2,1,0:T(8,128)(2,1)S(1)}, bf16[21,16,128]{2,1,0:T(8,128)(2,1)S(1)}, u32[]{:S(2)}, u32[]{:S(2)}) collective-permute-start(bf16[21,16,128]{2,1,0:T(8,128)(2,1)S(1)} %get-tuple-element.24), channel_id=1, source_target_pairs={{0,96},{16,112},{32,64},{48,80},{64,32},{80,48},{96,0},{112,16},{1... | collective-permute-start | bytes 258056 | tf_op jit(solution)/shard_map/ppermute | solution.py:460
  22.9 5.5 %collective-permute-start.6 = (bf16[21,16,128]{2,1,0:T(8,128)(2,1)S(1)}, bf16[21,16,128]{2,1,0:T(8,128)(2,1)S(1)}, u32[]{:S(2)}, u32[]{:S(2)}) collective-permute-start(bf16[21,16,128]{2,1,0:T(8,128)(2,1)S(1)} %get-tuple-element.25), channel_id=1, source_target_pairs={{0,112},{16,96},{32,80},{48,64},{64,48},{80,32},{96,16},{112,0},{1... | collective-permute-start | bytes 258056 | tf_op jit(solution)/shard_map/ppermute | solution.py:460
  32.7 21.8 %copy-start.7 = (bf16[64,64]{1,0:T(8,128)(2,1)S(1)}, bf16[64,64]{1,0:T(8,128)(2,1)}, u32[]{:S(2)}) copy-start(bf16[64,64]{1,0:T(8,128)(2,1)} %final_interp.1) | copy-start | bytes 24580
  32.7 21.8 %all-to-all-start.1 = ((bf16[16,8,16,128]{3,2,1,0:T(8,128)(2,1)}), bf16[16,8,16,128]{3,2,1,0:T(8,128)(2,1)S(1)}, u32[]{:S(2)}, u32[]{:S(2)}) async-start(bf16[16,8,16,128]{3,2,1,0:T(8,128)(2,1)} %bitcast.5), calls=%async_computation.1 | async-start | bytes 1048576 | tf_op jit(solution)/shard_map/all_to_all | solution.py:470
  43.4 0.8 %copy-start.4 = (f32[128,64]{0,1:T(8,128)S(1)}, f32[128,64]{0,1:T(8,128)}, u32[]{:S(2)}) copy-start(f32[128,64]{0,1:T(8,128)} %param.17) | copy-start | bytes 98308
  44.1 0.8 %copy-start.5 = (f32[8192]{0:T(1024)S(1)}, f32[8192]{0:T(1024)}, u32[]{:S(2)}) copy-start(f32[8192]{0:T(1024)} %param.19) | copy-start | bytes 98308

commit v2 on v1

--- a/solution.py
+++ b/solution.py
@@ -242,11 +242,33 @@
         put_weights(weights.at[4 + j], [interp[6 + j, 0], interp[6 + j, 1]])
 
 
+def near_kernel(*refs):
+    received = refs[:4]
+    interp, out, coeffs, tables, left, weights = refs[4:]
+    early = [
+        jnp.concatenate([received[d][16 + p].astype(F32) for d in range(4)], 0) for p in (0, 1, 3)
+    ]
+    for j in range(2):
+        theta = early[j] + with_partner(both(early[2], j), 16 * 2**j)
+        put_trig(theta, tables.at[j])
+        put_weights(weights.at[j], [interp[3 + j, 0], interp[3 + j, 1]])
+
+    def send(slot, value):
+        out[slot >> 4, slot & 15] = value
+
+    for j, load, store in (
+        (0, lambda slot: received[slot >> 4][slot & 15], storer(coeffs)),
+        (1, loader(coeffs), send),
+    ):
+        pairs = pairs_of(range(64), lambda slot: slot ^ 16 * 2**j)
+        level(pairs, load, lambda slot: slot, tables.at[j], weights.at[j], left, store)
+
+
 def middle_kernel(
     part, *refs
 ):
     received = refs[:8]
-    angles, late_tables, weights, out, coeffs, spare, tables, left = refs[8:]
+    near, angles, late_tables, weights, out, coeffs, spare, tables, left = refs[8:]
     count = 8 * len(part)
     size = 8 * count
     early = []
@@ -260,7 +282,11 @@
     late = lambda p: angles[:, 128 * p : 128 * p + 128].astype(F32)
     pending = both(early[3], 0)
     for j in range(3):
-        put_trig(early[j] + with_partner(pending, count * 2**j), tables.at[j])
+        theta = early[j] + with_partner(pending, count * 2**j)
+        if j < 2:
+            put_trig(theta[64:128], tables.at[j, 64:128])
+        else:
+            put_trig(theta, tables.at[j])
         pending = both(early[3 + (j + 1) // 2], (j + 1) % 2)
     perm = permutation(size, lambda rows: (rows & 7) * count + (rows >> 3))
     pending = jnp.dot(perm, pending.astype(BF16), preferred_element_type=F32)
@@ -275,10 +301,15 @@
     slots = range(size)
     stores = [storer(coeffs), storer(spare)]
     loads = [loader(coeffs), loader(spare)]
-    for j in range(3):
+    far = [slot for slot in slots if slot & 4]
+
+    def halfway(slot):
+        return spare[slot] if slot & 4 else near[slot & 7, slot >> 3]
+
+    for j, load in enumerate((arrived, loads[0], halfway)):
         level(
-            pairs_of(slots, lambda slot: slot ^ 2**j),
-            arrived if j == 0 else loads[(j + 1) % 2],
+            pairs_of(far if j < 2 else slots, lambda slot: slot ^ 2**j),
+            load,
             turned_row,
             tables.at[j],
             weights.at[j],
@@ -460,13 +491,21 @@
         lax.ppermute(piece, "src", [(i, i ^ k) for i in range(8)]) if k else piece
         for k, piece in enumerate(sent)
     ]
+    near = call(
+        near_kernel,
+        "near",
+        [whole(None)] * 5,
+        shape_of(4, 16, 16, 128),
+        [pltpu.VMEM((64, 16, 128), BF16), pltpu.VMEM((2, 64, 512), F32), left]
+        + [pltpu.VMEM((2, 256, 128), BF16)],
+    )(*received[:4], level_interp)
     sent = call(
         functools.partial(middle_kernel, part),
         "middle",
-        [whole(None)] * 11,
+        [whole(None)] * 12,
         shape_of(128, 16, 128),
         [tiles, tiles, pltpu.VMEM((4, 128, 512), F32), left],
-    )(*received, angles, late_tables, weights)
+    )(*received, near, angles, late_tables, weights)
     received = lax.all_to_all(
         sent.reshape(16, 8, 16, 128), "tgt", split_axis=0, concat_axis=0, tiled=True
     )

time: 57.5 us -> 57 us (level)
  waiting for transfers between devices: 13.4 us -> 12.2 us
  Pallas kernels: 12.1 us -> 12.9 us
    ppermute x7, waiting for transfers between devices: 4.45 us -> 3.25 us  [shards(): lax.ppermute(piece, 'src', [(i, i ^ k) for i in range(8)])]
    pallas_call x1 -> x2, Pallas kernels: 4.28 us -> 5.09 us  [the longest x1 3.94 us: shards(): call(functools.partial(middle_kernel, part), 'middle', [whole(None)] * 12...]
  transfers between devices with their start and end apart: 9 -> 9, of which waited for: 4 -> 3; matrix products, arithmetic and copies ran while one was open for 0% -> 0% of each run, Pallas kernels for 6% -> 8%
where the time goes in v2:
time: 57 us; the launch traced here: 56.5 us
  starting transfers between devices  29.8 us (52%)
  Pallas kernels  12.9 us (23%)
  waiting for transfers between devices  12.2 us (21%)
  local copies, waits for them, and re-layouts  1.54 us (3%)
    all_to_all x1, starting transfers between devices, shards(): lax.all_to_all(sent.reshape(16, 8, 16, 128), 'tgt', split_axis=0, concat_...  10.7 us
    ppermute x7, starting transfers between devices, shards(): lax.ppermute(piece, 'src', [(i, i ^ k) for i in range(8)])  9.97 us
    all_to_all x1, starting transfers between devices, shards(): lax.all_to_all(angles.reshape(16, 8, 896), 'tgt', split_axis=0, concat_ax...  9.13 us
    all_to_all x1, waiting for transfers between devices, shards(): lax.all_to_all(sent.reshape(16, 8, 16, 128), 'tgt', split_axis=0, concat_...  8.96 us
    pallas_call x1, Pallas kernels, shards(): call(functools.partial(middle_kernel, part), 'middle', [whole(None)] * 12...  3.94 us
    ppermute x7, waiting for transfers between devices, shards(): lax.ppermute(piece, 'src', [(i, i ^ k) for i in range(8)])  3.25 us
    pallas_call x1, Pallas kernels, shards(): call(target_kernel, 'target_side', [whole(None)] * 5, shape_of(2, 16, 819...  2.49 us
    pallas_call x1, Pallas kernels, shards(): call(angle_kernel, 'angles', [levels(2, 3), levels(2, 4), pl.BlockSpec((2...  2.1 us
  transfers between devices with their start and end apart: 9, of which 3 were waited for; matrix products, arithmetic and copies ran while one was open for 0% of the time, Pallas kernels for 8%

profile of v2, /device:TPU:1, one launch (start us, length us, event | category | flops | bytes accessed | tf_op | source)
XLA Modules:
  0.0 56.5 jit_solution(16926675853209439231)
XLA Ops:
  0.0 2.1 %angles.1 = bf16[128,896]{1,0:T(8,128)(2,1)} custom-call(f32[13,3,64,128]{3,2,1,0:T(8,128)} %bitcast.8, f32[13,3,64,128]{3,2,1,0:T(8,128)} %bitcast.9, f32[2,64,128]{2,1,0:T(8,128)} %bitcast.18), custom_call_target="tpu_custom_call" | custom-call | tf_op jit(solution)/shard_map/angles/pallas_call | solution.py:447
  2.1 9.1 %all-to-all-start = ((bf16[16,8,896]{2,1,0:T(8,128)(2,1)}), bf16[16,8,896]{2,1,0:T(8,128)(2,1)S(1)}, u32[]{:S(2)}, u32[]{:S(2)}) async-start(bf16[16,8,896]{2,1,0:T(8,128)(2,1)} %bitcast.17), calls=%async_computation | async-start | bytes 458752 | tf_op jit(solution)/shard_map/all_to_all | solution.py:457
  11.3 0.0 copy-start.8
  11.3 1.9 %source_side.1 = (bf16[21,16,128]{2,1,0:T(8,128)(2,1)S(1)}, bf16[21,16,128]{2,1,0:T(8,128)(2,1)S(1)}, bf16[21,16,128]{2,1,0:T(8,128)(2,1)S(1)}, bf16[21,16,128]{...) custom-call(f32[16,8192]{1,0:T(8,128)S(1)} %copy-done.2, ...), custom_call_target="tpu_custom_call" | custom-call | tf_op jit(solution)/shard_map/source_side/pallas_call | solution.py:481
  13.2 1.4 %collective-permute-start = (bf16[21,16,128]{2,1,0:T(8,128)(2,1)S(1)}, bf16[21,16,128]{2,1,0:T(8,128)(2,1)S(1)}, u32[]{:S(2)}, u32[]{:S(2)}) collective-permute-start(bf16[21,16,128]{2,1,0:T(8,128)(2,1)S(1)} %get-tuple-element.19), channel_id=1, source_target_pairs={{0,16},{16,0},{32,48},{48,32},{64,80},{80,64},{96,112},{112,96},{1... | collective-permute-start | bytes 258056 | tf_op jit(solution)/shard_map/ppermute | solution.py:491
  14.6 2.6 %collective-permute-start.1 = (bf16[21,16,128]{2,1,0:T(8,128)(2,1)S(1)}, bf16[21,16,128]{2,1,0:T(8,128)(2,1)S(1)}, u32[]{:S(2)}, u32[]{:S(2)}) collective-permute-start(bf16[21,16,128]{2,1,0:T(8,128)(2,1)S(1)} %get-tuple-element.20), channel_id=1, source_target_pairs={{0,32},{16,48},{32,0},{48,16},{64,96},{80,112},{96,64},{112,80},{1... | collective-permute-start | bytes 258056 | tf_op jit(solution)/shard_map/ppermute | solution.py:491
  17.2 0.7 %collective-permute-start.3 = (bf16[21,16,128]{2,1,0:T(8,128)(2,1)S(1)}, bf16[21,16,128]{2,1,0:T(8,128)(2,1)S(1)}, u32[]{:S(2)}, u32[]{:S(2)}) collective-permute-start(bf16[21,16,128]{2,1,0:T(8,128)(2,1)S(1)} %get-tuple-element.22), channel_id=1, source_target_pairs={{0,64},{16,80},{32,96},{48,112},{64,0},{80,16},{96,32},{112,48},{1... | collective-permute-start | bytes 258056 | tf_op jit(solution)/shard_map/ppermute | solution.py:491
  18.0 0.5 collective-permute-start.4
  18.4 4.3 %collective-permute-start.5 = (bf16[21,16,128]{2,1,0:T(8,128)(2,1)S(1)}, bf16[21,16,128]{2,1,0:T(8,128)(2,1)S(1)}, u32[]{:S(2)}, u32[]{:S(2)}) collective-permute-start(bf16[21,16,128]{2,1,0:T(8,128)(2,1)S(1)} %get-tuple-element.24), channel_id=1, source_target_pairs={{0,96},{16,112},{32,64},{48,80},{64,32},{80,48},{96,0},{112,16},{1... | collective-permute-start | bytes 258056 | tf_op jit(solution)/shard_map/ppermute | solution.py:491
  22.7 0.0 collective-permute-done.1.refs_2_
  22.7 0.4 collective-permute-start.6
  23.2 0.7 %collective-permute-done.2.refs_3_ = bf16[21,16,128]{2,1,0:T(8,128)(2,1)S(1)} collective-permute-done((bf16[21,16,128]{2,1,0:T(8,128)(2,1)S(1)}, bf16[21,16,128]{2,1,0:T(8,128)(2,1)S(1)}, u32[]{:S(2)}, u32[]{:S(2)}) %collective-permute-start.2) | collective-permute-done | bytes 86048 | tf_op jit(solution)/shard_map/ppermute | solution.py:491
  23.9 1.1 %near.1.refs_8_ = bf16[4,16,16,128]{3,2,1,0:T(8,128)(2,1)S(1)} custom-call(bf16[21,16,128]{2,1,0:T(8,128)(2,1)S(1)} %get-tuple-element.18.refs_0_, bf16[21,16,128]{2,1,0:T(8,128)(2,1)S(1)} %collective-permute-done.refs_1_, bf16[21,16,128]{2,1,0:T(8,128)(2,1)S(1)} %collective-permute-done.1.refs_2_, bf16[21,16,128]{2,1,0:T(8,128)(2,1)S(1)} %collective-permute-done.2.refs_3_, ...), custom_call_target="tpu_custom_call" | custom-call | tf_op jit(solution)/shard_map/near/pallas_call | solution.py:494
  25.1 0.0 all-to-all-done
  25.1 0.7 %late_tables.1 = (f32[4,128,512]{2,1,0:T(8,128)S(1)}, bf16[8,256,128]{2,1,0:T(8,128)(2,1)S(1)}) custom-call(bf16[128,896]{1,0:T(8,128)(2,1)S(1)} %bitcast.12, bf16[13,2,64,64]{3,2,1,0:T(8,128)(2,1)S(1)} %copy-done.1, bf16[64,64]{1,0:T(8,128)(2,1)S(1)} %copy-done.8), custom_call_target="tpu_custom_call" | custom-call | tf_op jit(solution)/shard_map/late_tables/pallas_call | solution.py:460
  25.7 0.0 collective-permute-done.3.refs_4_
  25.8 2.5 %collective-permute-done.6.refs_7_ = bf16[21,16,128]{2,1,0:T(8,128)(2,1)S(1)} collective-permute-done((bf16[21,16,128]{2,1,0:T(8,128)(2,1)S(1)}, bf16[21,16,128]{2,1,0:T(8,128)(2,1)S(1)}, u32[]{:S(2)}, u32[]{:S(2)}) %collective-permute-start.6) | collective-permute-done | bytes 86048 | tf_op jit(solution)/shard_map/ppermute | solution.py:491
  28.3 3.9 %middle.1 = bf16[128,16,128]{2,1,0:T(8,128)(2,1)} custom-call(bf16[21,16,128]{2,1,0:T(8,128)(2,1)S(1)} %get-tuple-element.18.refs_0_, bf16[21,16,128]{2,1,0:T(8,128)(2,1)S(1)} %collective-permute-done.refs_1_, bf16[21,16,128]{2,1,0:T(8,128)(2,1)S(1)} %collective-permute-done.1.refs_2_, bf16[21,16,128]{2,1,0:T(8,128)(2,1)S(1)} %collective-permute-done.2.refs_3_, ...), custom_call_target="tpu_custom_call" | custom-call | tf_op jit(solution)/shard_map/middle/pallas_call | solution.py:502
  32.2 10.7 %all-to-all-start.1 = ((bf16[16,8,16,128]{3,2,1,0:T(8,128)(2,1)}), bf16[16,8,16,128]{3,2,1,0:T(8,128)(2,1)S(1)}, u32[]{:S(2)}, u32[]{:S(2)}) async-start(bf16[16,8,16,128]{3,2,1,0:T(8,128)(2,1)} %bitcast.5), calls=%async_computation.1 | async-start | bytes 1048576 | tf_op jit(solution)/shard_map/all_to_all | solution.py:509
  42.9 0.8 %copy-done.4 = f32[128,64]{0,1:T(8,128)S(1)} copy-done((f32[128,64]{0,1:T(8,128)S(1)}, f32[128,64]{0,1:T(8,128)}, u32[]{:S(2)}) %copy-start.4) | copy-done | bytes 32792
  43.7 0.8 %copy-done.5 = f32[8192]{0:T(1024)S(1)} copy-done((f32[8192]{0:T(1024)S(1)}, f32[8192]{0:T(1024)}, u32[]{:S(2)}) %copy-start.5) | copy-done | bytes 32792
  44.4 0.7 %target_tables.1 = (f32[4,128,512]{2,1,0:T(8,128)S(1)}, bf16[3,256,128]{2,1,0:T(8,128)(2,1)S(1)}, f32[64,256]{1,0:T(8,128)S(1)}) custom-call(f32[13,3,64,128]{3,2,1,0:T(8,128)S(1)} %bitcast.11, f32[64,128]{1,0:T(8,128)S(1)} %bitcast.15, bf16[13,2,64,64]{3,2,1,0:T(8,128)(2,1)S(1)} %copy-done.1, f32[64,128]{1,0:T(8,128)S(1)} %bitcast.16), custom_call_target="tpu_custom_call" | custom-call | tf_op jit(solution)/shard_map/target_tables/pallas_call | solution.py:467
  45.1 9.0 %all-to-all-done.1.received = bf16[16,8,16,128]{3,2,1,0:T(8,128)(2,1)S(1)} async-done(((bf16[16,8,16,128]{3,2,1,0:T(8,128)(2,1)}), bf16[16,8,16,128]{3,2,1,0:T(8,128)(2,1)S(1)}, u32[]{:S(2)}, u32[]{:S(2)}) %all-to-all-start.1) | async-done | bytes 524320 | tf_op jit(solution)/shard_map/all_to_all | solution.py:509
  54.0 2.5 %target_side.1 = f32[2,16,8192]{2,1,0:T(8,128)} custom-call(bf16[16,8,16,128]{3,2,1,0:T(8,128)(2,1)S(1)} %all-to-all-done.1.received, f32[4,128,512]{2,1,0:T(8,128)S(1)} %get-tuple-element.28.tables, bf16[3,256,128]{2,1,0:T(8,128)(2,1)S(1)} %get-tuple-element.29.weights, f32[64,256]{1,0:T(8,128)S(1)} %get-tuple-element.30.trig, bf16[64,64]{1,0:T(8,128)(2,1)S(1)} %copy-done.7), custom_call_target="tpu_custom_call" | custom-call | tf_op jit(solution)/shard_map/target_side/pallas_call | solution.py:512
  (19 shorter events, 0.0 us)
Async XLA Ops:
  0.0 11.3 %copy-start = (f32[13,3,128,64]{2,3,1,0:T(8,128)S(1)}, f32[13,3,128,64]{2,3,1,0:T(8,128)}, u32[]{:S(2)}) copy-start(f32[13,3,128,64]{2,3,1,0:T(8,128)} %param.14) | copy-start | bytes 3833860
  0.0 11.3 %copy-start.1 = (bf16[13,2,64,64]{3,2,1,0:T(8,128)(2,1)S(1)}, bf16[13,2,64,64]{3,2,1,0:T(8,128)(2,1)}, u32[]{:S(2)}) copy-start(bf16[13,2,64,64]{3,2,1,0:T(8,128)(2,1)} %interp.5) | copy-start | bytes 638980
  0.0 11.3 %copy-start.2 = (f32[16,8192]{1,0:T(8,128)S(1)}, f32[16,8192]{1,0:T(8,128)}, u32[]{:S(2)}) copy-start(f32[16,8192]{1,0:T(8,128)} %values.1) | copy-start | bytes 1572868
  0.0 11.3 %copy-start.3 = (f32[8192]{0:T(1024)S(1)}, f32[8192]{0:T(1024)}, u32[]{:S(2)}) copy-start(f32[8192]{0:T(1024)} %param.11) | copy-start | bytes 98308
  0.0 11.3 %copy-start.6 = (bf16[64,64]{1,0:T(8,128)(2,1)S(1)}, bf16[64,64]{1,0:T(8,128)(2,1)}, u32[]{:S(2)}) copy-start(bf16[64,64]{1,0:T(8,128)(2,1)} %leaf.1) | copy-start | bytes 24580
  2.1 22.9 %all-to-all-start = ((bf16[16,8,896]{2,1,0:T(8,128)(2,1)}), bf16[16,8,896]{2,1,0:T(8,128)(2,1)S(1)}, u32[]{:S(2)}, u32[]{:S(2)}) async-start(bf16[16,8,896]{2,1,0:T(8,128)(2,1)} %bitcast.17), calls=%async_computation | async-start | bytes 458752 | tf_op jit(solution)/shard_map/all_to_all | solution.py:457
  11.3 13.8 %copy-start.8 = (bf16[64,64]{1,0:T(8,128)(2,1)S(1)}, bf16[64,64]{1,0:T(8,128)(2,1)}, u32[]{:S(2)}) copy-start(bf16[64,64]{1,0:T(8,128)(2,1)} %middle_interp.1) | copy-start | bytes 24580
  13.2 5.2 %collective-permute-start = (bf16[21,16,128]{2,1,0:T(8,128)(2,1)S(1)}, bf16[21,16,128]{2,1,0:T(8,128)(2,1)S(1)}, u32[]{:S(2)}, u32[]{:S(2)}) collective-permute-start(bf16[21,16,128]{2,1,0:T(8,128)(2,1)S(1)} %get-tuple-element.19), channel_id=1, source_target_pairs={{0,16},{16,0},{32,48},{48,32},{64,80},{80,64},{96,112},{112,96},{1... | collective-permute-start | bytes 258056 | tf_op jit(solution)/shard_map/ppermute | solution.py:491
  14.6 8.1 %collective-permute-start.1 = (bf16[21,16,128]{2,1,0:T(8,128)(2,1)S(1)}, bf16[21,16,128]{2,1,0:T(8,128)(2,1)S(1)}, u32[]{:S(2)}, u32[]{:S(2)}) collective-permute-start(bf16[21,16,128]{2,1,0:T(8,128)(2,1)S(1)} %get-tuple-element.20), channel_id=1, source_target_pairs={{0,32},{16,48},{32,0},{48,16},{64,96},{80,112},{96,64},{112,80},{1... | collective-permute-start | bytes 258056 | tf_op jit(solution)/shard_map/ppermute | solution.py:491
  17.2 6.7 %collective-permute-start.2 = (bf16[21,16,128]{2,1,0:T(8,128)(2,1)S(1)}, bf16[21,16,128]{2,1,0:T(8,128)(2,1)S(1)}, u32[]{:S(2)}, u32[]{:S(2)}) collective-permute-start(bf16[21,16,128]{2,1,0:T(8,128)(2,1)S(1)} %get-tuple-element.21), channel_id=1, source_target_pairs={{0,48},{16,32},{32,16},{48,0},{64,112},{80,96},{96,80},{112,64},{1... | collective-permute-start | bytes 258056 | tf_op jit(solution)/shard_map/ppermute | solution.py:491
  17.2 8.5 %collective-permute-start.3 = (bf16[21,16,128]{2,1,0:T(8,128)(2,1)S(1)}, bf16[21,16,128]{2,1,0:T(8,128)(2,1)S(1)}, u32[]{:S(2)}, u32[]{:S(2)}) collective-permute-start(bf16[21,16,128]{2,1,0:T(8,128)(2,1)S(1)} %get-tuple-element.22), channel_id=1, source_target_pairs={{0,64},{16,80},{32,96},{48,112},{64,0},{80,16},{96,32},{112,48},{1... | collective-permute-start | bytes 258056 | tf_op jit(solution)/shard_map/ppermute | solution.py:491
  18.0 7.8 %collective-permute-start.4 = (bf16[21,16,128]{2,1,0:T(8,128)(2,1)S(1)}, bf16[21,16,128]{2,1,0:T(8,128)(2,1)S(1)}, u32[]{:S(2)}, u32[]{:S(2)}) collective-permute-start(bf16[21,16,128]{2,1,0:T(8,128)(2,1)S(1)} %get-tuple-element.23), channel_id=1, source_target_pairs={{0,80},{16,64},{32,112},{48,96},{64,16},{80,0},{96,48},{112,32},{1... | collective-permute-start | bytes 258056 | tf_op jit(solution)/shard_map/ppermute | solution.py:491
  18.4 7.3 %collective-permute-start.5 = (bf16[21,16,128]{2,1,0:T(8,128)(2,1)S(1)}, bf16[21,16,128]{2,1,0:T(8,128)(2,1)S(1)}, u32[]{:S(2)}, u32[]{:S(2)}) collective-permute-start(bf16[21,16,128]{2,1,0:T(8,128)(2,1)S(1)} %get-tuple-element.24), channel_id=1, source_target_pairs={{0,96},{16,112},{32,64},{48,80},{64,32},{80,48},{96,0},{112,16},{1... | collective-permute-start | bytes 258056 | tf_op jit(solution)/shard_map/ppermute | solution.py:491
  22.7 5.5 %collective-permute-start.6 = (bf16[21,16,128]{2,1,0:T(8,128)(2,1)S(1)}, bf16[21,16,128]{2,1,0:T(8,128)(2,1)S(1)}, u32[]{:S(2)}, u32[]{:S(2)}) collective-permute-start(bf16[21,16,128]{2,1,0:T(8,128)(2,1)S(1)} %get-tuple-element.25), channel_id=1, source_target_pairs={{0,112},{16,96},{32,80},{48,64},{64,48},{80,32},{96,16},{112,0},{1... | collective-permute-start | bytes 258056 | tf_op jit(solution)/shard_map/ppermute | solution.py:491
  32.2 21.8 %copy-start.7 = (bf16[64,64]{1,0:T(8,128)(2,1)S(1)}, bf16[64,64]{1,0:T(8,128)(2,1)}, u32[]{:S(2)}) copy-start(bf16[64,64]{1,0:T(8,128)(2,1)} %final_interp.1) | copy-start | bytes 24580
  32.2 21.8 %all-to-all-start.1 = ((bf16[16,8,16,128]{3,2,1,0:T(8,128)(2,1)}), bf16[16,8,16,128]{3,2,1,0:T(8,128)(2,1)S(1)}, u32[]{:S(2)}, u32[]{:S(2)}) async-start(bf16[16,8,16,128]{3,2,1,0:T(8,128)(2,1)} %bitcast.5), calls=%async_computation.1 | async-start | bytes 1048576 | tf_op jit(solution)/shard_map/all_to_all | solution.py:509
  42.9 0.8 %copy-start.4 = (f32[128,64]{0,1:T(8,128)S(1)}, f32[128,64]{0,1:T(8,128)}, u32[]{:S(2)}) copy-start(f32[128,64]{0,1:T(8,128)} %param.17) | copy-start | bytes 98308
  43.7 0.8 %copy-start.5 = (f32[8192]{0:T(1024)S(1)}, f32[8192]{0:T(1024)}, u32[]{:S(2)}) copy-start(f32[8192]{0:T(1024)} %param.19) | copy-start | bytes 98308
